TPU v7x, 32 devices: a whole 2x2x4 slice. The times are simulated.
32 devices in a mesh: lev: 2 (over y), hor: 16 (over z, x, core).
Axes of the slice: x: 2, y: 2, z: 4, core: 2. Of those that a mesh axis runs over, the one named last changes fastest.
Arguments:
- heat_field: float32 [64, 512, 512], P('lev', 'hor'), may hold values from -6 to 6
- saline_field: float32 [64, 512, 512], P('lev', 'hor'), may hold values from -6 to 6
- updraft_speed: float32 [64, 512, 512], P('lev', 'hor'), may hold values from -3 to 3
- heat_mixing_rates: float32 [64], P('lev'), may hold values from 0.05 to 1
- saline_mixing_rates: float32 [64], P('lev'), may hold values from 0.05 to 1
- cross_mixing_rates: float32 [64], P('lev'), may hold values from 0.2 to 1
Outputs:
- updated_heat_field: float32 [64, 512, 512], P('lev', 'hor')
- salt_out: float32 [64, 512, 512], P('lev', 'hor')
All inputs are finite; a program needn't handle non-finite values.
Results may differ from a plain program's by a relative error of at most 0.000073.
Values sent between devices are 32-bit elements; how exact they have to be, the bound alone decides.
A program may use at most 128 MiB of HBM per device.

v0:
```python
import math

import jax
import jax.numpy as jnp
from jax import lax
from jax.sharding import PartitionSpec as P

highest = lax.Precision.HIGHEST
buoyancy = 0.5
advective_number = 0.25


def extended_2(block, sides, width):
    for axis, dim in sides:
        count = lax.axis_size(axis)
        forward = [(i, i + 1) for i in range(count - 1)]
        backward = [(target, source) for source, target in forward]
        low = lax.ppermute(
            lax.slice_in_dim(block, block.shape[dim] - width, None, axis=dim), axis, forward
        )
        high = lax.ppermute(lax.slice_in_dim(block, 0, width, axis=dim), axis, backward)
        block = jnp.concatenate([low, block, high], axis=dim)
    return block


def wave_angles(left, right, length):
    product = left[:, None] * right[None, :] % length
    return 2.0 * math.pi / length * product.astype(jnp.float32)


def slot_waves(block, within, slot_count, length):
    paired = slot_count // 2
    upper_wave = (length - paired * block - (within - paired)) % length
    waves = jnp.where(within < paired, paired * block + within, upper_wave)
    waves = jnp.where((block == 0) & (within == paired), length // 2, waves)
    return waves


def signed_wave(waves, length):
    return jnp.where(waves < length // 2, waves, waves - length).astype(jnp.float32)


def contract(form, left, right):
    return jnp.einsum(form, left, right, precision=highest)


def complex_product(real_part, imag_part, form, cos_table, sin_table, sign):
    real_out = contract(form, real_part, cos_table) - sign * contract(form, imag_part, sin_table)
    imag_out = contract(form, imag_part, cos_table) + sign * contract(form, real_part, sin_table)
    return (real_out, imag_out)


def shards(
    heat_field,
    saline_field,
    updraft_speed,
    heat_mixing_rates,
    saline_mixing_rates,
    cross_mixing_rates,
):
    number_of_layers, number_of_lines, number_of_stacks = heat_field.shape
    parts = lax.axis_size("hor")
    block_index = lax.axis_index("hor")
    length_x = number_of_lines * parts
    slot_count = number_of_stacks // parts
    paired = slot_count // 2
    every_slot = jnp.arange(number_of_stacks)
    all_waves = slot_waves(
        every_slot // slot_count, every_slot % slot_count, slot_count, number_of_stacks
    )
    angle_y = wave_angles(jnp.arange(number_of_stacks), all_waves, number_of_stacks)
    north_cos_lookup = jnp.cos(angle_y).reshape(number_of_stacks, parts, slot_count)
    north_sin_lookup = jnp.sin(angle_y).reshape(number_of_stacks, parts, slot_count)
    x_points = jnp.arange(length_x)
    angle_x = wave_angles(x_points, x_points, length_x)
    cos_x = jnp.cos(angle_x)
    sin_x = jnp.sin(angle_x)
    within = jnp.arange(slot_count)
    wave_y = signed_wave(
        slot_waves(block_index, within, slot_count, number_of_stacks), number_of_stacks
    )
    wave_x = signed_wave(x_points, length_x)
    modulus = (wave_y[:, None] * wave_y[:, None] + wave_x[None, :] * wave_x[None, :]) / (
        length_x / 2.0 * (length_x / 2.0)
    )
    normalizing_factor = 1.0 / (length_x * number_of_stacks)

    def split_into_groups(array):
        return array.reshape(number_of_layers, parts, number_of_lines * slot_count)

    joint_real, joint_imag = complex_product(
        heat_field, saline_field, "uhq,qvj->uvhj", north_cos_lookup, north_sin_lookup, -1.0
    )
    pieces = (
        lax.all_to_all(
            split_into_groups(joint_real), "hor", split_axis=1, concat_axis=1, tiled=True
        ),
        lax.all_to_all(
            split_into_groups(joint_imag), "hor", split_axis=1, concat_axis=1, tiled=True
        ),
    )
    count = pieces[0].shape[0]
    shaped = [piece.reshape(count, length_x, slot_count) for piece in pieces]
    results = []
    results.extend(complex_product(shaped[0], shaped[1], "zxj,xm->zjm", cos_x, sin_x, -1.0))
    spec_real, spec_imag = tuple(results)
    keep_self = ((block_index == 0) & ((within == 0) | (within == paired)))[None, :, None]

    def mirror(array):
        swapped = jnp.concatenate([array[:, paired:], array[:, :paired]], axis=1)
        swapped = jnp.where(keep_self, array, swapped)
        return jnp.roll(jnp.flip(swapped, 2), 1, 2)

    mirror_real = mirror(spec_real)
    mirror_imag = mirror(spec_imag)
    heat_nonimag_share = 0.5 * (spec_real + mirror_real)
    temp_imag = 0.5 * (spec_imag - mirror_imag)
    salt_real = 0.5 * (spec_imag + mirror_imag)
    salt_imag = 0.5 * (mirror_real - spec_real)
    diag_temp = 1.0 + heat_mixing_rates[:, None, None] * modulus[None]
    diag_salt = 1.0 + saline_mixing_rates[:, None, None] * modulus[None]
    cross_term = cross_mixing_rates[:, None, None] * modulus[None]
    determinant = diag_temp * diag_salt + cross_term * cross_term
    new_temp_real = (diag_salt * heat_nonimag_share - cross_term * salt_real) / determinant
    new_temp_imag = (diag_salt * temp_imag - cross_term * salt_imag) / determinant
    new_salt_real = (diag_temp * salt_real + cross_term * heat_nonimag_share) / determinant
    new_salt_imag = (diag_temp * salt_imag + cross_term * temp_imag) / determinant
    real_out, imag_out = complex_product(
        new_temp_real - new_salt_imag,
        new_temp_imag + new_salt_real,
        "zjm,mx->zxj",
        cos_x,
        sin_x,
        1.0,
    )
    back_real = split_into_groups(real_out)
    back_imag = split_into_groups(imag_out)
    pieces = (
        lax.all_to_all(back_real, "hor", split_axis=1, concat_axis=1, tiled=True),
        lax.all_to_all(back_imag, "hor", split_axis=1, concat_axis=1, tiled=True),
    )
    count = pieces[0].shape[0]
    real_part = pieces[0].reshape(count, parts, number_of_lines, slot_count)
    imag_part = pieces[1].reshape(count, parts, number_of_lines, slot_count)
    real_out, imag_out = complex_product(
        real_part, imag_part, "zbxj,ybj->zxy", north_cos_lookup, north_sin_lookup, 1.0
    )
    filtered_heat_field = real_out * normalizing_factor
    filtered_saline_field = imag_out * normalizing_factor
    joined_layers = jnp.stack([filtered_heat_field, filtered_saline_field, updraft_speed])
    extended = extended_2(joined_layers, (("lev", 1),), 1)
    lower = extended[:, :-1]
    upper = extended[:, 1:]
    interface_flow = 0.5 * (lower[2] + upper[2]) + buoyancy * 0.5 * (
        lower[0] + upper[0] - (lower[1] + upper[1])
    )
    face_global = lax.axis_index("lev") * number_of_layers + jnp.arange(number_of_layers + 1) - 1
    total_levels = number_of_layers * lax.axis_size("lev")
    open_face = ((face_global >= 0) & (face_global <= total_levels - 2))[:, None, None]
    upward_flow = jnp.maximum(interface_flow, 0.0)
    downward_flow = jnp.minimum(interface_flow, 0.0)
    heat_transport = jnp.where(open_face, upward_flow * lower[0] + downward_flow * upper[0], 0.0)
    flux_salt = jnp.where(open_face, upward_flow * lower[1] + downward_flow * upper[1], 0.0)
    updated_heat_field = filtered_heat_field - advective_number * (
        heat_transport[1:] - heat_transport[:-1]
    )
    salt_out = filtered_saline_field - advective_number * (flux_salt[1:] - flux_salt[:-1])
    return (updated_heat_field, salt_out)


def solution(mesh):
    in_specs = (
        P("lev", "hor", None),
        P("lev", "hor", None),
        P("lev", "hor", None),
        P("lev"),
        P("lev"),
        P("lev"),
    )
    out_specs = (P("lev", "hor", None), P("lev", "hor", None))
    return jax.shard_map(shards, mesh=mesh, in_specs=in_specs, out_specs=out_specs, check_vma=False)
```

profile of v0, /device:TPU:10, one launch (start us, length us, event | category | flops | bytes accessed | tf_op | source)
XLA Modules:
  0.0 493.8 jit_solution(12389758087010161159)
XLA Ops:
  0.7 19.4 %fusion.20 = f32[16,32,32,32]{3,1,2,0:T(8,128)S(1)} fusion(f32[32,32,512]{2,1,0:T(8,128)} %param.7, s32[16,32]{1,0:T(8,128)S(1)} %fusion.90), kind=kOutput, calls=%fused_computation.44 | convolution fusion | flops 3224895488 | bytes 4196352 | tf_op jit(solution)/shard_map/uhq,qvj->uvhj/dot_general | solution.py:44
  20.1 23.4 %add_bitcast_fusion = f32[32,16,32,32]{2,3,0,1:T(8,128)} fusion(f32[16,32,32,32]{3,1,2,0:T(8,128)S(1)} %fusion.20, f32[32,32,512]{2,1,0:T(8,128)S(1)} %copy-done, s32[16,32]{1,0:T(8,128)S(1)} %fusion.90), kind=kOutput, calls=%fused_computation | convolution fusion | flops 3225944064 | bytes 6293504 | tf_op jit(solution)/shard_map/uhq,qvj->uvhj/dot_general | solution.py:44
  43.5 9.0 %copy.43 = f32[32,16,32,32]{3,2,0,1:T(8,128)} copy(f32[32,16,32,32]{2,3,0,1:T(8,128)} %add_bitcast_fusion) | data formatting | bytes 4194304 | tf_op jit(solution)/shard_map/reshape | solution.py:89
  52.4 7.7 %reshape.281 = f32[32,16,1024]{2,0,1:T(8,128)} reshape(f32[32,16,32,32]{3,2,0,1:T(8,128)} %copy.43) | data formatting | bytes 4194304 | tf_op jit(solution)/shard_map/reshape | solution.py:89
  60.1 16.8 %all-to-all-start.1 = ((f32[32,16,1024]{2,0,1:T(8,128)}), f32[32,16,1024]{2,0,1:T(8,128)}, u32[]{:S(2)}, u32[]{:S(2)}) async-start(f32[32,16,1024]{2,0,1:T(8,128)} %reshape.281), calls=%async_computation.1 | async-start | bytes 4194304 | tf_op jit(solution)/shard_map/all_to_all | solution.py:98
  76.9 17.4 %fusion.24 = f32[16,32,32,32]{3,1,2,0:T(8,128)S(1)} fusion(f32[32,32,512]{2,1,0:T(8,128)S(1)} %copy-done, s32[16,32]{1,0:T(8,128)S(1)} %fusion.90), kind=kOutput, calls=%fused_computation.48 | convolution fusion | flops 3224895488 | bytes 4196352 | tf_op jit(solution)/shard_map/uhq,qvj->uvhj/dot_general | solution.py:44
  94.3 23.8 %subtract_bitcast_fusion = f32[32,16,32,32]{2,3,0,1:T(8,128)} fusion(f32[16,32,32,32]{3,1,2,0:T(8,128)S(1)} %fusion.24, f32[32,32,512]{2,1,0:T(8,128)S(1)} %copy-done.12, s32[16,32]{1,0:T(8,128)S(1)} %fusion.90), kind=kOutput, calls=%fused_computation.1 | convolution fusion | flops 3225944064 | bytes 6293504 | tf_op jit(solution)/shard_map/uhq,qvj->uvhj/dot_general | solution.py:44
  118.1 9.0 %copy.42 = f32[32,16,32,32]{3,2,0,1:T(8,128)} copy(f32[32,16,32,32]{2,3,0,1:T(8,128)} %subtract_bitcast_fusion) | data formatting | bytes 4194304 | tf_op jit(solution)/shard_map/reshape | solution.py:89
  127.1 7.7 %reshape.280 = f32[32,16,1024]{2,0,1:T(8,128)} reshape(f32[32,16,32,32]{3,2,0,1:T(8,128)} %copy.42) | data formatting | bytes 4194304 | tf_op jit(solution)/shard_map/reshape | solution.py:89
  134.8 6.0 %all-to-all-start = ((f32[32,16,1024]{2,0,1:T(8,128)}), f32[32,16,1024]{2,0,1:T(8,128)}, u32[]{:S(2)}, u32[]{:S(2)}) async-start(f32[32,16,1024]{2,0,1:T(8,128)} %reshape.280), calls=%async_computation | async-start | bytes 4194304 | tf_op jit(solution)/shard_map/all_to_all | solution.py:95
  140.9 0.1 add_multiply_fusion.2
  140.9 2.8 copy.22
  143.8 5.0 %reshape.263 = f32[32,512,32]{2,1,0:T(8,128)} reshape(f32[32,16,1024]{2,1,0:T(8,128)S(1)} %copy.22) | data formatting | bytes 4194304 | tf_op jit(solution)/shard_map/reshape | solution.py:103
  148.8 23.8 %fusion.53 = f32[32,32,512]{2,1,0:T(8,128)} fusion(f32[32,512,32]{2,1,0:T(8,128)} %reshape.263), kind=kOutput, calls=%fused_computation.96 | convolution fusion | flops 3224895488 | bytes 4194304 | tf_op jit(solution)/shard_map/zxj,xm->zjm/dot_general | solution.py:44
  172.6 15.6 %all-to-all-done = f32[32,16,1024]{2,0,1:T(8,128)} async-done(((f32[32,16,1024]{2,0,1:T(8,128)}), f32[32,16,1024]{2,0,1:T(8,128)}, u32[]{:S(2)}, u32[]{:S(2)}) %all-to-all-start) | async-done | bytes 2097184 | tf_op jit(solution)/shard_map/all_to_all | solution.py:95
  188.2 2.8 copy.18
  191.0 4.8 reshape.261
  195.8 22.4 %fusion.55 = f32[32,32,512]{2,1,0:T(8,128)S(1)} fusion(f32[32,512,32]{2,1,0:T(8,128)} %reshape.261), kind=kOutput, calls=%fused_computation.98 | convolution fusion | flops 3224895488 | bytes 4194304 | tf_op jit(solution)/shard_map/zxj,xm->zjm/dot_general | solution.py:44
  218.2 22.5 %multiply_add_fusion.1 = f32[32,32,512]{2,1,0:T(8,128)S(1)} fusion(f32[32,32,512]{2,1,0:T(8,128)S(1)} %copy-done.10, f32[32,512,32]{2,1,0:T(8,128)} %reshape.261), kind=kOutput, calls=%fused_computation.56 | convolution fusion | flops 3225944064 | bytes 6291456 | tf_op jit(solution)/shard_map/zxj,xm->zjm/dot_general | solution.py:44
  240.7 19.2 %multiply_subtract_fusion = f32[32,32,512]{2,1,0:T(8,128)S(1)} fusion(f32[32,32,512]{2,1,0:T(8,128)S(1)} %fusion.55, f32[32,512,32]{2,1,0:T(8,128)S(1)} %bitcast.137), kind=kOutput, calls=%fused_computation.58 | convolution fusion | flops 3225944064 | bytes 6291456 | tf_op jit(solution)/shard_map/zxj,xm->zjm/dot_general | solution.py:44
  260.0 0.6 fusion.171
  260.6 0.9 copy-done.2
  261.5 1.2 maximum_select_fusion.1
  262.8 1.9 slice.105
  264.7 0.1 slice.104
  264.8 2.0 slice.109
  266.8 4.2 reverse.4
  271.0 3.5 slice.160
  274.5 4.2 reverse.5
  278.7 2.3 slice.161
  281.1 0.5 copy-done.11
  281.5 3.0 fusion.11
  284.5 8.3 %fusion.49 = f32[512,32,32]{0,2,1:T(8,128)S(1)} fusion(f32[32,32,512]{2,1,0:T(8,128)S(1)} %get-tuple-element.4), kind=kOutput, calls=%fused_computation.92 | convolution fusion | flops 3224895488 | bytes 4194304 | tf_op jit(solution)/shard_map/zjm,mx->zxj/dot_general | solution.py:44
  292.9 8.5 %add_bitcast_fusion.1 = f32[32,512,32]{1,2,0:T(8,128)S(1)} fusion(f32[512,32,32]{0,2,1:T(8,128)S(1)} %fusion.49, f32[32,32,512]{2,1,0:T(8,128)S(1)} %get-tuple-element.5), kind=kOutput, calls=%fused_computation.50 | convolution fusion | flops 3225419776 | bytes 6291456 | tf_op jit(solution)/shard_map/zjm,mx->zxj/dot_general | solution.py:44
  301.4 4.7 copy.29
  306.2 6.6 %reshape.266 = f32[32,16,1024]{2,1,0:T(8,128)S(1)} reshape(f32[32,512,32]{2,1,0:T(8,128)} %copy.29) | data formatting | bytes 4194304 | tf_op jit(solution)/shard_map/reshape | solution.py:89
  312.8 2.6 copy.30
  315.4 5.6 %all-to-all-start.3 = ((f32[32,16,1024]{2,0,1:T(8,128)}), f32[32,16,1024]{2,0,1:T(8,128)}, u32[]{:S(2)}, u32[]{:S(2)}) async-start(f32[32,16,1024]{2,0,1:T(8,128)} %copy.30), calls=%async_computation.3 | async-start | bytes 4194304 | tf_op jit(solution)/shard_map/all_to_all | solution.py:140
  321.0 8.3 %fusion.51 = f32[512,32,32]{0,2,1:T(8,128)S(1)} fusion(f32[32,32,512]{2,1,0:T(8,128)S(1)} %copy-done.16), kind=kOutput, calls=%fused_computation.94 | convolution fusion | flops 3224895488 | bytes 4194304 | tf_op jit(solution)/shard_map/zjm,mx->zxj/dot_general | solution.py:44
  329.3 8.4 %subtract_bitcast_fusion.1 = f32[32,512,32]{1,2,0:T(8,128)S(1)} fusion(f32[512,32,32]{0,2,1:T(8,128)S(1)} %fusion.51, f32[32,32,512]{2,1,0:T(8,128)S(1)} %copy-done.14), kind=kOutput, calls=%fused_computation.51 | convolution fusion | flops 3225419776 | bytes 6291456 | tf_op jit(solution)/shard_map/zjm,mx->zxj/dot_general | solution.py:44
  337.7 4.7 copy.26
  342.4 6.6 %reshape.264 = f32[32,16,1024]{2,1,0:T(8,128)S(1)} reshape(f32[32,512,32]{2,1,0:T(8,128)} %copy.26) | data formatting | bytes 4194304 | tf_op jit(solution)/shard_map/reshape | solution.py:89
  349.1 2.5 copy.27
  351.6 16.6 %all-to-all-done.3 = f32[32,16,1024]{2,0,1:T(8,128)} async-done(((f32[32,16,1024]{2,0,1:T(8,128)}), f32[32,16,1024]{2,0,1:T(8,128)}, u32[]{:S(2)}, u32[]{:S(2)}) %all-to-all-start.3) | async-done | bytes 2097184 | tf_op jit(solution)/shard_map/all_to_all | solution.py:140
  368.2 5.6 %all-to-all-start.2 = ((f32[32,16,1024]{2,0,1:T(8,128)}), f32[32,16,1024]{2,0,1:T(8,128)}, u32[]{:S(2)}, u32[]{:S(2)}) async-start(f32[32,16,1024]{2,0,1:T(8,128)} %copy.27), calls=%async_computation.2 | async-start | bytes 4194304 | tf_op jit(solution)/shard_map/all_to_all | solution.py:139
  373.8 2.8 copy.31
  376.6 4.9 reshape.267
  381.4 18.4 %fusion.37 = f32[32,32,512,1]{2,1,3,0:T(8,128)} fusion(f32[32,16,32,32]{3,2,1,0:T(8,128)} %reshape.267, s32[16,32]{1,0:T(8,128)S(1)} %fusion.90), kind=kOutput, calls=%fused_computation.80 | convolution fusion | flops 3224895488 | bytes 4196352 | tf_op jit(solution)/shard_map/zbxj,ybj->zxy/dot_general | solution.py:44
  399.8 21.1 %all-to-all-done.2 = f32[32,16,1024]{2,0,1:T(8,128)} async-done(((f32[32,16,1024]{2,0,1:T(8,128)}), f32[32,16,1024]{2,0,1:T(8,128)}, u32[]{:S(2)}, u32[]{:S(2)}) %all-to-all-start.2) | async-done | bytes 2097184 | tf_op jit(solution)/shard_map/all_to_all | solution.py:139
  421.0 2.8 copy.28
  423.8 4.8 reshape.265
  428.6 18.0 %fusion.39 = f32[32,32,512,1]{2,1,3,0:T(8,128)S(1)} fusion(f32[32,16,32,32]{3,2,1,0:T(8,128)} %reshape.265, s32[16,32]{1,0:T(8,128)S(1)} %fusion.90), kind=kOutput, calls=%fused_computation.82 | convolution fusion | flops 3224895488 | bytes 4196352 | tf_op jit(solution)/shard_map/zbxj,ybj->zxy/dot_general | solution.py:44
  446.6 10.9 %fusion.18 = f32[32,32,512]{2,1,0:T(8,128)S(1)} fusion(f32[32,32,512,1]{2,1,3,0:T(8,128)S(1)} %copy-done.20, f32[32,16,32,32]{3,2,1,0:T(8,128)S(1)} %copy-done.9, s32[16,32]{1,0:T(8,128)S(1)} %fusion.90), kind=kOutput, calls=%fused_computation.41 | convolution fusion | flops 3225944064 | bytes 6293504 | tf_op jit(solution)/shard_map/zbxj,ybj->zxy/dot_general | solution.py:44
  457.6 11.2 %fusion.19 = f32[32,32,512]{2,1,0:T(8,128)S(1)} fusion(f32[32,32,512,1]{2,1,3,0:T(8,128)S(1)} %fusion.39, f32[32,16,32,32]{3,2,1,0:T(8,128)S(1)} %bitcast.145, s32[16,32]{1,0:T(8,128)S(1)} %fusion.90), kind=kOutput, calls=%fused_computation.43 | convolution fusion | flops 3225944064 | bytes 6293504 | tf_op jit(solution)/shard_map/zbxj,ybj->zxy/dot_general | solution.py:44
  468.9 3.4 collective-permute-start
  472.4 1.3 collective-permute-start.1
  473.7 3.3 collective-permute-done
  477.0 4.1 collective-permute-done.1
  481.1 4.7 pad_maximum_fusion
  485.9 2.1 add_select_fusion
  488.0 1.9 fusion.15
  489.9 0.9 add_select_fusion.1
  490.8 0.7 copy-done.5
  491.5 1.9 fusion.17
  (57 shorter events, 0.3 us)
Async XLA Ops:
  0.6 19.4 %copy-start = (f32[32,32,512]{2,1,0:T(8,128)S(1)}, f32[32,32,512]{2,1,0:T(8,128)}, u32[]{:S(2)}) copy-start(f32[32,32,512]{2,1,0:T(8,128)} %param.6) | copy-start | bytes 6291460
  60.1 74.7 %all-to-all-start.1 = ((f32[32,16,1024]{2,0,1:T(8,128)}), f32[32,16,1024]{2,0,1:T(8,128)}, u32[]{:S(2)}, u32[]{:S(2)}) async-start(f32[32,16,1024]{2,0,1:T(8,128)} %reshape.281), calls=%async_computation.1 | async-start | bytes 4194304 | tf_op jit(solution)/shard_map/all_to_all | solution.py:98
  76.9 17.4 %copy-start.12 = (f32[32,32,512]{2,1,0:T(8,128)S(1)}, f32[32,32,512]{2,1,0:T(8,128)}, u32[]{:S(2)}) copy-start(f32[32,32,512]{2,1,0:T(8,128)} %param.7) | copy-start | bytes 6291460
  134.8 53.4 %all-to-all-start = ((f32[32,16,1024]{2,0,1:T(8,128)}), f32[32,16,1024]{2,0,1:T(8,128)}, u32[]{:S(2)}, u32[]{:S(2)}) async-start(f32[32,16,1024]{2,0,1:T(8,128)} %reshape.280), calls=%async_computation | async-start | bytes 4194304 | tf_op jit(solution)/shard_map/all_to_all | solution.py:95
  195.8 22.4 %copy-start.10 = (f32[32,32,512]{2,1,0:T(8,128)S(1)}, f32[32,32,512]{2,1,0:T(8,128)}, u32[]{:S(2)}) copy-start(f32[32,32,512]{2,1,0:T(8,128)} %fusion.53) | copy-start | bytes 6291460
  195.8 44.9 %slice-start = ((s8[8388608]{0:T(1024)(128)(4,1)}), s8[4194304]{0:T(1024)(128)(4,1)S(1)}, s32[]{:S(2)}) async-start(s8[8388608]{0:T(1024)(128)(4,1)} %bitcast.136), calls=%async_computation.4 | async-start | bytes 8388608
  218.2 22.5 %slice-start.1 = ((s8[8388608]{0:T(1024)(128)(4,1)}), s8[4194304]{0:T(1024)(128)(4,1)S(1)}, s32[]{:S(2)}) async-start(s8[8388608]{0:T(1024)(128)(4,1)} %bitcast.136), calls=%async_computation.5 | async-start | bytes 8388608
  260.0 1.5 copy-start.2
  274.5 6.5 %copy-start.17 = (f32[32]{0:T(128)S(1)}, f32[32]{0:T(128)}, u32[]{:S(2)}) copy-start(f32[32]{0:T(128)} %param.9) | copy-start | bytes 388
  274.5 6.6 %copy-start.18 = (f32[32]{0:T(128)S(1)}, f32[32]{0:T(128)}, u32[]{:S(2)}) copy-start(f32[32]{0:T(128)} %param.11) | copy-start | bytes 388
  274.5 6.6 %copy-start.19 = (f32[32]{0:T(128)S(1)}, f32[32]{0:T(128)}, u32[]{:S(2)}) copy-start(f32[32]{0:T(128)} %param.10) | copy-start | bytes 388
  278.7 2.4 copy-start.3
  278.7 2.9 copy-start.11
  284.5 8.4 %copy-start.13 = (f32[32,32,512]{2,1,0:T(8,128)}, f32[32,32,512]{2,1,0:T(8,128)S(1)}, u32[]{:S(2)}) copy-start(f32[32,32,512]{2,1,0:T(8,128)S(1)} %get-tuple-element.4) | copy-start | bytes 6291460
  284.5 8.4 %copy-start.15 = (f32[32,32,512]{2,1,0:T(8,128)}, f32[32,32,512]{2,1,0:T(8,128)S(1)}, u32[]{:S(2)}) copy-start(f32[32,32,512]{2,1,0:T(8,128)S(1)} %get-tuple-element.5) | copy-start | bytes 6291460
  315.4 5.6 %copy-start.16 = (f32[32,32,512]{2,1,0:T(8,128)S(1)}, f32[32,32,512]{2,1,0:T(8,128)}, u32[]{:S(2)}) copy-start(f32[32,32,512]{2,1,0:T(8,128)} %copy-done.15) | copy-start | bytes 6291460
  315.4 52.8 %all-to-all-start.3 = ((f32[32,16,1024]{2,0,1:T(8,128)}), f32[32,16,1024]{2,0,1:T(8,128)}, u32[]{:S(2)}, u32[]{:S(2)}) async-start(f32[32,16,1024]{2,0,1:T(8,128)} %copy.30), calls=%async_computation.3 | async-start | bytes 4194304 | tf_op jit(solution)/shard_map/all_to_all | solution.py:140
  321.0 8.3 %copy-start.14 = (f32[32,32,512]{2,1,0:T(8,128)S(1)}, f32[32,32,512]{2,1,0:T(8,128)}, u32[]{:S(2)}) copy-start(f32[32,32,512]{2,1,0:T(8,128)} %copy-done.13) | copy-start | bytes 6291460
  368.2 52.8 %all-to-all-start.2 = ((f32[32,16,1024]{2,0,1:T(8,128)}), f32[32,16,1024]{2,0,1:T(8,128)}, u32[]{:S(2)}, u32[]{:S(2)}) async-start(f32[32,16,1024]{2,0,1:T(8,128)} %copy.27), calls=%async_computation.2 | async-start | bytes 4194304 | tf_op jit(solution)/shard_map/all_to_all | solution.py:139
  428.6 18.1 %copy-start.9 = (f32[32,16,32,32]{3,2,1,0:T(8,128)S(1)}, f32[32,16,32,32]{3,2,1,0:T(8,128)}, u32[]{:S(2)}) copy-start(f32[32,16,32,32]{3,2,1,0:T(8,128)} %reshape.265) | copy-start | bytes 6291460
  428.6 18.1 %copy-start.20 = (f32[32,32,512,1]{2,1,3,0:T(8,128)S(1)}, f32[32,32,512,1]{2,1,3,0:T(8,128)}, u32[]{:S(2)}) copy-start(f32[32,32,512,1]{2,1,3,0:T(8,128)} %fusion.37) | copy-start | bytes 6291460
  428.6 29.0 %slice-start.2 = ((s8[8388608]{0:T(1024)(128)(4,1)}), s8[4194304]{0:T(1024)(128)(4,1)S(1)}, s32[]{:S(2)}) async-start(s8[8388608]{0:T(1024)(128)(4,1)} %bitcast.144), calls=%async_computation.6 | async-start | bytes 8388608
  446.6 11.0 %slice-start.3 = ((s8[8388608]{0:T(1024)(128)(4,1)}), s8[4194304]{0:T(1024)(128)(4,1)S(1)}, s32[]{:S(2)}) async-start(s8[8388608]{0:T(1024)(128)(4,1)} %bitcast.144), calls=%async_computation.7 | async-start | bytes 8388608
  457.6 11.2 %copy-start.6 = (f32[32,32,512]{2,1,0:T(8,128)}, f32[32,32,512]{2,1,0:T(8,128)S(1)}, u32[]{:S(2)}) copy-start(f32[32,32,512]{2,1,0:T(8,128)S(1)} %fusion.18) | copy-start | bytes 6291460
  457.6 11.2 %copy-start.8 = (f32[32,32,512]{2,1,0:T(8,128)S(1)}, f32[32,32,512]{2,1,0:T(8,128)}, u32[]{:S(2)}) copy-start(f32[32,32,512]{2,1,0:T(8,128)} %param.8) | copy-start | bytes 6291460
  468.9 12.2 %copy-start.4 = (f32[32,32,512]{2,1,0:T(8,128)}, f32[32,32,512]{2,1,0:T(8,128)S(1)}, u32[]{:S(2)}) copy-start(f32[32,32,512]{2,1,0:T(8,128)S(1)} %fusion.19) | copy-start | bytes 6291460
  468.9 8.0 %collective-permute-start = (f32[3,1,32,512]{3,2,1,0:T(8,128)S(1)}, f32[3,1,32,512]{3,2,1,0:T(8,128)S(1)}, u32[]{:S(2)}, u32[]{:S(2)}) collective-permute-start(f32[3,1,32,512]{3,2,1,0:T(8,128)S(1)} %get-tuple-element.9), channel_id=1, source_target_pairs={{0,16},{1,17},{2,18},{3,19},{4,20},{5,21},{6,22},{7,23},{8,24},{9,... | collective-permute-start | bytes 589832 | tf_op jit(solution)/shard_map/ppermute | solution.py:18
  472.4 8.7 %collective-permute-start.1 = (f32[3,1,32,512]{3,2,1,0:T(8,128)S(1)}, f32[3,1,32,512]{3,2,1,0:T(8,128)S(1)}, u32[]{:S(2)}, u32[]{:S(2)}) collective-permute-start(f32[3,1,32,512]{3,2,1,0:T(8,128)S(1)} %get-tuple-element.8), channel_id=1, source_target_pairs={{16,0},{17,1},{18,2},{19,3},{20,4},{21,5},{22,6},{23,7},{24,8},{25... | collective-permute-start | bytes 589832 | tf_op jit(solution)/shard_map/ppermute | solution.py:21
  485.8 2.2 copy-start.7
  489.9 1.6 copy-start.5
  491.5 1.9 copy-start.1
where the time goes:
time: 504 us; the launch traced here: 494 us
  matrix products  264 us (52%)
  local copies, waits for them, and re-layouts  113 us (22%)
  waiting for transfers between devices  60.7 us (12%)
  starting transfers between devices  38.7 us (8%)
  other arithmetic  15.9 us (3%)
    dot_general x16, matrix products, contract(): return jnp.einsum(form, left, right, precision=highest)  264 us
    reshape x8, local copies, waits for them, and re-layouts, split_into_groups(): return array.reshape(number_of_layers, parts, number_of_lines * slot_count)  51.7 us
    all_to_all x1, waiting for transfers between devices, shards(): lax.all_to_all(back_real, 'hor', split_axis=1, concat_axis=1, tiled=True)  21.1 us
    all_to_all x1, starting transfers between devices, shards(): lax.all_to_all(split_into_groups(joint_imag), 'hor', split_axis=1, concat...  16.8 us
    all_to_all x1, waiting for transfers between devices, shards(): lax.all_to_all(back_imag, 'hor', split_axis=1, concat_axis=1, tiled=True)  16.6 us
    unnamed x54, local copies, waits for them, and re-layouts  16.4 us
    all_to_all x1, waiting for transfers between devices, shards(): lax.all_to_all(split_into_groups(joint_real), 'hor', split_axis=1, concat...  15.6 us
  transfers between devices with their start and end apart: 6, of which 5 were waited for; matrix products, arithmetic and copies ran while one was open for 30% of the time, Pallas kernels for 0%

commit v1 on v0

v1 whole, which is shorter than its diff:
```python
import functools
import math

import jax
import jax.numpy as jnp
import ml_dtypes
import numpy as np
from jax import lax
from jax.experimental import pallas as pl
from jax.experimental.pallas import tpu as pltpu
from jax.sharding import PartitionSpec as P

MESH = pl.DeviceIdType.MESH
LANES = 128
buoyancy = 0.5
advective_number = 0.25


def wave_table(length):
    half = length // 2
    waves = []
    for parity in range(2):
        k = np.repeat(2 * np.arange(half // 2) + parity, 2)
        if parity == 0:
            k[1] = half
        waves.append(k)
    return waves


def basis(length):
    half = length // 2
    points = np.arange(half)
    out = []
    for parity, k in enumerate(wave_table(length)):
        angle = 2.0 * math.pi / length * ((k[:, None] * points[None, :]) % length)
        rows = np.where(np.arange(half)[:, None] % 2 == 0, np.cos(angle), np.sin(angle))
        rows = rows * math.sqrt(2.0 / length)
        if parity == 0:
            rows[0] = 1.0 / math.sqrt(length)
            rows[1] = np.cos(math.pi * points) / math.sqrt(length)
        out.append(rows)
    return out


def thirds(matrix, axis):
    high = matrix.astype(ml_dtypes.bfloat16)
    low = (matrix - high.astype(np.float64)).astype(ml_dtypes.bfloat16)
    return np.concatenate([high, high, low], axis=axis)


def split3(x, axis):
    high = x.astype(jnp.bfloat16)
    low = (x - high.astype(jnp.float32)).astype(jnp.bfloat16)
    return jnp.concatenate([high, low, high], axis=axis)


def dot(a, b):
    return jnp.dot(a, b, preferred_element_type=jnp.float32)


def block_transpose(tiles, width, lane):
    count = len(tiles)
    tiles = list(tiles)
    step = count // 2
    while step >= 1:
        keep = (lane // width) % (2 * step) < step
        for i in range(count):
            if i & step == 0:
                a, b = tiles[i], tiles[i + step]
                tiles[i] = jnp.where(keep, a, pltpu.roll(b, step * width, 1))
                tiles[i + step] = jnp.where(
                    keep, pltpu.roll(a, LANES - step * width, 1), b
                )
        step //= 2
    return tiles


def kernel(
    parts, levs, slots,
    heat, salt, speed, rate_t, rate_s, rate_c, fwd_y, inv_y, fwd_x, inv_x, wx2, wy2,
    out_t, out_s,
    send, recv, back_send, back_recv, ext,
    send_sem, recv_sem, back_send_sem, back_recv_sem, speed_sem, halo_send, halo_recv,
):
    layers, rows, length_y = heat.shape
    pack = LANES // slots
    chunks = layers // pack
    half_y = length_y // 2
    length_x = rows * parts
    half_x = length_x // 2
    me = lax.axis_index("hor")
    lev = lax.axis_index("lev")
    has_low = lev > 0
    has_high = lev < levs - 1

    def peer(d):
        return lax.rem(me + d, parts)

    barrier = pltpu.get_barrier_semaphore()

    def greet(d, carry):
        pl.semaphore_signal(barrier, inc=1, device_id={"hor": peer(d)}, device_id_type=MESH)
        return carry

    lax.fori_loop(1, parts, greet, 0)

    @pl.when(has_low)
    def _():
        pl.semaphore_signal(barrier, inc=1, device_id={"lev": lev - 1}, device_id_type=MESH)

    @pl.when(has_high)
    def _():
        pl.semaphore_signal(barrier, inc=1, device_id={"lev": lev + 1}, device_id_type=MESH)

    speed_copy = pltpu.make_async_copy(speed, ext.at[2, pl.ds(1, layers)], speed_sem)
    speed_copy.start()

    def halo_up(kind):
        first, count = (2, 1) if kind == 0 else (0, 2)
        return pltpu.make_async_remote_copy(
            src_ref=ext.at[pl.ds(first, count), layers],
            dst_ref=ext.at[pl.ds(first, count), 0],
            send_sem=halo_send.at[0, kind],
            recv_sem=halo_recv.at[0, kind],
            device_id={"lev": lev + 1},
            device_id_type=MESH,
        )

    def halo_down(kind):
        first, count = (2, 1) if kind == 0 else (0, 2)
        return pltpu.make_async_remote_copy(
            src_ref=ext.at[pl.ds(first, count), 1],
            dst_ref=ext.at[pl.ds(first, count), layers + 1],
            send_sem=halo_send.at[1, kind],
            recv_sem=halo_recv.at[1, kind],
            device_id={"lev": lev - 1},
            device_id_type=MESH,
        )

    def send_halo(kind):
        @pl.when(has_high)
        def _():
            halo_up(kind).start()

        @pl.when(has_low)
        def _():
            halo_down(kind).start()

    def wait_halo(kind):
        @pl.when(has_high)
        def _():
            halo_up(kind).wait_send()
            halo_down(kind).wait_recv()

        @pl.when(has_low)
        def _():
            halo_down(kind).wait_send()
            halo_up(kind).wait_recv()

    @pl.when(jnp.logical_not(has_low))
    def _():
        ext[:, 0] = jnp.zeros((3, rows, length_y), jnp.float32)

    @pl.when(jnp.logical_not(has_high))
    def _():
        ext[:, layers + 1] = jnp.zeros((3, rows, length_y), jnp.float32)

    def chunk_of(i):
        return lax.rem(i + chunks - 1, chunks)

    def lane_of(shape):
        return lax.broadcasted_iota(jnp.int32, shape, 1)

    def exchange(source, target, s_sem, r_sem, c):
        def one(d, carry):
            q = peer(d)
            pltpu.make_async_remote_copy(
                src_ref=source.at[c, q],
                dst_ref=target.at[c, me],
                send_sem=s_sem.at[c],
                recv_sem=r_sem.at[c],
                device_id={"hor": q},
                device_id_type=MESH,
            ).start()
            return carry

        lax.fori_loop(1, parts, one, 0)
        target[c, me] = source[c, me]

    def wait_all(ref, sem, c):
        view = ref.at[c, pl.ds(0, parts - 1)]
        pltpu.make_async_copy(view, view, sem.at[c]).wait()

    def north(c):
        level = pl.ds(c * pack, pack)
        x = jnp.concatenate(
            [ref[level].reshape(pack * rows, length_y) for ref in (heat, salt)], axis=0
        )
        a, b = x[:, :half_y], x[:, half_y:]
        spectra = [
            dot(split3(a + b, 1), fwd_y[0]).reshape(2, pack, rows, half_y),
            dot(split3(a - b, 1), fwd_y[1]).reshape(2, pack, rows, half_y),
        ]
        lane = lane_of((rows, LANES))
        for parity in range(2):
            for tile in range(half_y // LANES):
                q0 = (parity * (half_y // LANES) + tile) * pack
                cols = slice(tile * LANES, (tile + 1) * LANES)
                for f in range(2):
                    tiles = [spectra[parity][f, z, :, cols] for z in range(pack)]
                    for i, t in enumerate(block_transpose(tiles, slots, lane)):
                        send[c, q0 + i, f] = t

    def east(c):
        both = jnp.concatenate(
            [recv[c, :, f].reshape(length_x, LANES) for f in range(2)], axis=1
        )
        a, b = both[:half_x], both[half_x:]
        block = lane_of((1, LANES)) // slots
        rates = []
        for ref in (rate_t, rate_s, rate_c):
            row = jnp.full((1, LANES), ref[c * pack], jnp.float32)
            for z in range(1, pack):
                row = jnp.where(block == z, ref[c * pack + z], row)
            rates.append(row)
        waves_y = wy2[me]
        result = []
        for parity, x in enumerate((a + b, a - b)):
            spec = dot(fwd_x[parity], split3(x, 0))
            t, s = spec[:, :LANES], spec[:, LANES:]
            modulus = wx2[parity] + waves_y
            diag_t = 1.0 + rates[0] * modulus
            diag_s = 1.0 + rates[1] * modulus
            cross = rates[2] * modulus
            inverse = 1.0 / (diag_t * diag_s + cross * cross)
            new = jnp.concatenate(
                [(diag_s * t - cross * s) * inverse, (diag_t * s + cross * t) * inverse], axis=1
            )
            result.append(dot(inv_x[parity], split3(new, 0)))
        for k, x in enumerate((result[0] + result[1], result[0] - result[1])):
            for f in range(2):
                back_send[c, pl.ds(k * (parts // 2), parts // 2), f] = x[
                    :, f * LANES : (f + 1) * LANES
                ].reshape(parts // 2, rows, LANES)

    def south(c):
        lane = lane_of((rows, LANES))
        ends = []
        for parity in range(2):
            fields = []
            columns = []
            for f in range(2):
                by_tile = []
                for tile in range(half_y // LANES):
                    q0 = (parity * (half_y // LANES) + tile) * pack
                    tiles = [back_recv[c, q0 + i, f] for i in range(pack)]
                    by_tile.append(block_transpose(tiles, slots, lane))
                for z in range(pack):
                    columns.append(jnp.concatenate([t[z] for t in by_tile], axis=1))
            x = jnp.concatenate(columns, axis=0)
            ends.append(dot(split3(x, 1), inv_y[parity]))
        for k, x in enumerate((ends[0] + ends[1], ends[0] - ends[1])):
            ext[pl.ds(0, 2), pl.ds(1 + c * pack, pack), :, pl.ds(k * half_y, half_y)] = x.reshape(
                2, pack, rows, half_y
            )

    def advect(c):
        base = c * pack

        def face(j, r):
            low_t, high_t = ext[0, j, r], ext[0, j + 1, r]
            low_s, high_s = ext[1, j, r], ext[1, j + 1, r]
            flow = 0.5 * (ext[2, j, r] + ext[2, j + 1, r]) + buoyancy * 0.5 * (
                (low_t + high_t) - (low_s + high_s)
            )
            shut = jnp.logical_or(
                jnp.logical_and(j == 0, jnp.logical_not(has_low)),
                jnp.logical_and(j == layers, jnp.logical_not(has_high)),
            )
            flow = flow * jnp.where(shut, 0.0, 1.0)
            up = jnp.maximum(flow, 0.0)
            down = jnp.minimum(flow, 0.0)
            return up * low_t + down * high_t, up * low_s + down * high_s

        for group in range(rows // 8):
            r = pl.ds(group * 8, 8)
            below = face(base, r)
            for z in range(pack):
                level = base + z
                above = face(level + 1, r)
                out_t[level, r] = ext[0, level + 1, r] - advective_number * (above[0] - below[0])
                out_s[level, r] = ext[1, level + 1, r] - advective_number * (above[1] - below[1])
                below = above

    c0 = chunk_of(0)
    north(c0)
    pl.semaphore_wait(
        barrier, parts - 1 + jnp.where(has_low, 1, 0) + jnp.where(has_high, 1, 0)
    )
    exchange(send, recv, send_sem, recv_sem, c0)

    def forward(i, carry):
        c = chunk_of(i)
        north(c)
        exchange(send, recv, send_sem, recv_sem, c)
        return carry

    lax.fori_loop(1, chunks, forward, 0)
    speed_copy.wait()
    send_halo(0)

    def middle(i, carry):
        c = chunk_of(i)
        wait_all(recv, recv_sem, c)
        east(c)
        exchange(back_send, back_recv, back_send_sem, back_recv_sem, c)
        return carry

    lax.fori_loop(0, chunks, middle, 0)

    def backward(i, carry):
        c = chunk_of(i)
        wait_all(back_recv, back_recv_sem, c)
        south(c)

        @pl.when(i == 1)
        def _():
            send_halo(1)

        @pl.when(i == 2)
        def _():
            wait_halo(0)
            wait_halo(1)

        @pl.when(i >= 2)
        def _():
            advect(c - 1)

        return carry

    lax.fori_loop(0, chunks, backward, 0)
    advect(chunks - 2)
    advect(chunks - 1)

    def drain(c, carry):
        wait_all(send, send_sem, c)
        wait_all(back_send, back_send_sem, c)
        return carry

    lax.fori_loop(0, chunks, drain, 0)


def shards(heat, salt, speed, rate_t, rate_s, rate_c):
    layers, rows, length_y = heat.shape
    parts = lax.axis_size("hor")
    levs = lax.axis_size("lev")
    length_x = rows * parts
    slots = length_y // parts
    pack = LANES // slots
    chunks = layers // pack
    rows_y, rows_x = basis(length_y), basis(length_x)
    fwd_y = np.stack([thirds(m.T, 0) for m in rows_y])
    inv_y = np.stack([thirds(m, 0) for m in rows_y])
    fwd_x = np.stack([thirds(m, 1) for m in rows_x])
    inv_x = np.stack([thirds(m.T, 1) for m in rows_x])
    scale = (length_x / 2.0) ** 2
    wx2 = np.stack([np.repeat((k * k / scale)[:, None], LANES, 1) for k in wave_table(length_x)])
    every = np.concatenate(wave_table(length_y)).reshape(parts, 1, slots)
    wy2 = np.tile(every * every / scale, (1, 1, pack))
    tables = [jnp.asarray(m) for m in (fwd_y, inv_y, fwd_x, inv_x)]
    tables += [jnp.asarray(m.astype(np.float32)) for m in (wx2, wy2)]
    vmem = pl.BlockSpec(memory_space=pltpu.VMEM)
    smem = pl.BlockSpec(memory_space=pltpu.SMEM)
    anywhere = pl.BlockSpec(memory_space=pl.ANY)
    block = pltpu.VMEM((chunks, parts, 2, rows, LANES), jnp.float32)
    sems = pltpu.SemaphoreType.DMA((chunks,))
    shape = jax.ShapeDtypeStruct(heat.shape, jnp.float32)
    return pl.pallas_call(
        functools.partial(kernel, parts, levs, slots),
        out_shape=(shape, shape),
        in_specs=[vmem, vmem, anywhere, smem, smem, smem] + [vmem] * 6,
        out_specs=(vmem, vmem),
        scratch_shapes=[
            block, block, block, block,
            pltpu.VMEM((3, layers + 2, rows, length_y), jnp.float32),
            sems, sems, sems, sems,
            pltpu.SemaphoreType.DMA,
            pltpu.SemaphoreType.DMA((2, 2)),
            pltpu.SemaphoreType.DMA((2, 2)),
        ],
        compiler_params=pltpu.CompilerParams(
            collective_id=0, has_side_effects=True, vmem_limit_bytes=58 * 2**20
        ),
    )(heat, salt, speed, rate_t, rate_s, rate_c, *tables)


def solution(mesh):
    field = P("lev", "hor", None)
    in_specs = (field, field, field, P("lev"), P("lev"), P("lev"))
    return jax.shard_map(
        shards, mesh=mesh, in_specs=in_specs, out_specs=(field, field), check_vma=False
    )
```

time: 504 us -> 198 us (0.39)
  the two profiles are of different devices: /device:TPU:10 before, /device:TPU:0 now
where the time goes in v1:
time: 198 us; the launch traced here: 196 us
  Pallas kernels  190 us (96%)
  local copies, waits for them, and re-layouts  4.66 us (2%)
    pallas_call x1, Pallas kernels, shards(): pl.pallas_call(functools.partial(kernel, parts, levs, slots), out_shape=(...  190 us
    unnamed x4, local copies, waits for them, and re-layouts  4.66 us

profile of v1, /device:TPU:0, one launch (start us, length us, event | category | flops | bytes accessed | tf_op | source)
XLA Modules:
  0.0 195.6 jit_solution(6030391408771863193)
XLA Ops:
  0.6 190.2 %shard_map.131 = (f32[32,32,512]{2,1,0:T(8,128)}, f32[32,32,512]{2,1,0:T(8,128)}) custom-call(f32[32,32,512]{2,1,0:T(8,128)} %heat.1, f32[32,32,512]{2,1,0:T(8,128)} %salt.1, f32[32,32,512]{2,1,0:T(8,128)} %speed.1, f32[32]{0:T(128)} %rate_t.1, f32[32]{0:T(128)} %rate_s.1, f32[32]{0:T(128)} %rate_c.1, bf16[2,768,256]{2,1,0:T(8,128)(2,1)} %constant.12.clone.fwd_y, ...), custom_call_target="tpu_custom_call" | custom-call | tf_op jit(solution)/shard_map/pallas_call | solution.py:378
  190.9 0.0 copy-start
  190.9 3.3 %copy.16 = f32[32,32,512]{2,1,0:T(8,128)} copy(f32[32,32,512]{2,1,0:T(8,128)} %get-tuple-element.4) | data formatting | bytes 4194304
  194.2 0.0 copy-done
  194.2 1.3 copy.17
Async XLA Ops:
  190.9 3.3 %copy-start = (f32[32,32,512]{2,1,0:T(8,128)S(1)}, f32[32,32,512]{2,1,0:T(8,128)}, u32[]{:S(2)}) copy-start(f32[32,32,512]{2,1,0:T(8,128)} %get-tuple-element.5) | copy-start | bytes 6291460

commit v2 on v1

--- a/solution.py
+++ b/solution.py
@@ -77,11 +77,14 @@
 
 def kernel(
     parts, levs, slots,
-    heat, salt, speed, rate_t, rate_s, rate_c, fwd_y, inv_y, fwd_x, inv_x, wx2, wy2,
-    out_t, out_s,
-    send, recv, back_send, back_recv, ext,
-    send_sem, recv_sem, back_send_sem, back_recv_sem, speed_sem, halo_send, halo_recv,
+    heat, salt, speed, rate_t, rate_s, rate_c, *rest
 ):
+    sources, rest = rest[:6], rest[6:]
+    filtered, speed_ends = rest[:2]
+    send, recv, back_send, back_recv, field, new, *tables = rest[2:14]
+    fwd_y, inv_y, fwd_x, inv_x, wx2, wy2 = tables
+    send_sem, recv_sem, back_send_sem, back_recv_sem = rest[14:18]
+    field_sem, new_sem, table_sem, halo_send, halo_recv = rest[18:]
     layers, rows, length_y = heat.shape
     pack = LANES // slots
     chunks = layers // pack
@@ -112,30 +115,53 @@
     def _():
         pl.semaphore_signal(barrier, inc=1, device_id={"lev": lev + 1}, device_id_type=MESH)
 
-    speed_copy = pltpu.make_async_copy(speed, ext.at[2, pl.ds(1, layers)], speed_sem)
-    speed_copy.start()
-
-    def halo_up(kind):
-        first, count = (2, 1) if kind == 0 else (0, 2)
+    def field_copy(f, c):
+        level = pl.ds(c * pack, pack)
+        return pltpu.make_async_copy(
+            (heat, salt)[f].at[level], field.at[f, level], field_sem.at[f, c]
+        )
+
+    def table_copy(k):
+        return pltpu.make_async_copy(sources[k], tables[k], table_sem.at[k])
+
+    def new_copy(c):
+        return pltpu.make_async_copy(
+            new.at[:, pl.ds(c * pack, pack)],
+            filtered.at[:, pl.ds(1 + c * pack, pack)],
+            new_sem.at[c],
+        )
+
+    def chunk_of(i):
+        return lax.rem(i + chunks - 1, chunks)
+
+    def read(i, carry):
+        field_copy(0, chunk_of(i)).start()
+        field_copy(1, chunk_of(i)).start()
+        return carry
+
+    table_copy(0).start()
+    lax.fori_loop(0, chunks, read, 0)
+    for k in range(1, len(tables)):
+        table_copy(k).start()
+
+    def halo(up, kind):
+        level, place = (layers - 1, 0) if up else (0, 1)
+        if kind == 0:
+            source, target = speed.at[level], speed_ends.at[place]
+        else:
+            source, target = new.at[:, level], filtered.at[:, place * (layers + 1)]
+        way = 0 if up else 1
         return pltpu.make_async_remote_copy(
-            src_ref=ext.at[pl.ds(first, count), layers],
-            dst_ref=ext.at[pl.ds(first, count), 0],
-            send_sem=halo_send.at[0, kind],
-            recv_sem=halo_recv.at[0, kind],
-            device_id={"lev": lev + 1},
+            src_ref=source,
+            dst_ref=target,
+            send_sem=halo_send.at[way, kind],
+            recv_sem=halo_recv.at[way, kind],
+            device_id={"lev": lev + 1 if up else lev - 1},
             device_id_type=MESH,
         )
 
-    def halo_down(kind):
-        first, count = (2, 1) if kind == 0 else (0, 2)
-        return pltpu.make_async_remote_copy(
-            src_ref=ext.at[pl.ds(first, count), 1],
-            dst_ref=ext.at[pl.ds(first, count), layers + 1],
-            send_sem=halo_send.at[1, kind],
-            recv_sem=halo_recv.at[1, kind],
-            device_id={"lev": lev - 1},
-            device_id_type=MESH,
-        )
+    halo_up = functools.partial(halo, True)
+    halo_down = functools.partial(halo, False)
 
     def send_halo(kind):
         @pl.when(has_high)
@@ -156,17 +182,6 @@
         def _():
             halo_down(kind).wait_send()
             halo_up(kind).wait_recv()
-
-    @pl.when(jnp.logical_not(has_low))
-    def _():
-        ext[:, 0] = jnp.zeros((3, rows, length_y), jnp.float32)
-
-    @pl.when(jnp.logical_not(has_high))
-    def _():
-        ext[:, layers + 1] = jnp.zeros((3, rows, length_y), jnp.float32)
-
-    def chunk_of(i):
-        return lax.rem(i + chunks - 1, chunks)
 
     def lane_of(shape):
         return lax.broadcasted_iota(jnp.int32, shape, 1)
@@ -194,7 +209,7 @@
     def north(c):
         level = pl.ds(c * pack, pack)
         x = jnp.concatenate(
-            [ref[level].reshape(pack * rows, length_y) for ref in (heat, salt)], axis=0
+            [field[f, level].reshape(pack * rows, length_y) for f in range(2)], axis=0
         )
         a, b = x[:, :half_y], x[:, half_y:]
         spectra = [
@@ -260,54 +275,32 @@
             x = jnp.concatenate(columns, axis=0)
             ends.append(dot(split3(x, 1), inv_y[parity]))
         for k, x in enumerate((ends[0] + ends[1], ends[0] - ends[1])):
-            ext[pl.ds(0, 2), pl.ds(1 + c * pack, pack), :, pl.ds(k * half_y, half_y)] = x.reshape(
+            new[:, pl.ds(c * pack, pack), :, pl.ds(k * half_y, half_y)] = x.reshape(
                 2, pack, rows, half_y
             )
 
-    def advect(c):
-        base = c * pack
-
-        def face(j, r):
-            low_t, high_t = ext[0, j, r], ext[0, j + 1, r]
-            low_s, high_s = ext[1, j, r], ext[1, j + 1, r]
-            flow = 0.5 * (ext[2, j, r] + ext[2, j + 1, r]) + buoyancy * 0.5 * (
-                (low_t + high_t) - (low_s + high_s)
-            )
-            shut = jnp.logical_or(
-                jnp.logical_and(j == 0, jnp.logical_not(has_low)),
-                jnp.logical_and(j == layers, jnp.logical_not(has_high)),
-            )
-            flow = flow * jnp.where(shut, 0.0, 1.0)
-            up = jnp.maximum(flow, 0.0)
-            down = jnp.minimum(flow, 0.0)
-            return up * low_t + down * high_t, up * low_s + down * high_s
-
-        for group in range(rows // 8):
-            r = pl.ds(group * 8, 8)
-            below = face(base, r)
-            for z in range(pack):
-                level = base + z
-                above = face(level + 1, r)
-                out_t[level, r] = ext[0, level + 1, r] - advective_number * (above[0] - below[0])
-                out_s[level, r] = ext[1, level + 1, r] - advective_number * (above[1] - below[1])
-                below = above
-
-    c0 = chunk_of(0)
-    north(c0)
+    def forward(i):
+        c = chunk_of(i)
+        field_copy(0, c).wait()
+        field_copy(1, c).wait()
+        north(c)
+        return c
+
+    table_copy(0).wait()
+    first = forward(0)
     pl.semaphore_wait(
         barrier, parts - 1 + jnp.where(has_low, 1, 0) + jnp.where(has_high, 1, 0)
     )
-    exchange(send, recv, send_sem, recv_sem, c0)
-
-    def forward(i, carry):
-        c = chunk_of(i)
-        north(c)
-        exchange(send, recv, send_sem, recv_sem, c)
-        return carry
-
-    lax.fori_loop(1, chunks, forward, 0)
-    speed_copy.wait()
+    exchange(send, recv, send_sem, recv_sem, first)
+
+    def outward(i, carry):
+        exchange(send, recv, send_sem, recv_sem, forward(i))
+        return carry
+
+    lax.fori_loop(1, chunks, outward, 0)
     send_halo(0)
+    for k in range(1, len(tables)):
+        table_copy(k).wait()
 
     def middle(i, carry):
         c = chunk_of(i)
@@ -322,32 +315,52 @@
         c = chunk_of(i)
         wait_all(back_recv, back_recv_sem, c)
         south(c)
+        new_copy(c).start()
 
         @pl.when(i == 1)
         def _():
             send_halo(1)
 
-        @pl.when(i == 2)
-        def _():
-            wait_halo(0)
-            wait_halo(1)
-
-        @pl.when(i >= 2)
-        def _():
-            advect(c - 1)
-
         return carry
 
     lax.fori_loop(0, chunks, backward, 0)
-    advect(chunks - 2)
-    advect(chunks - 1)
+    wait_halo(0)
+    wait_halo(1)
 
     def drain(c, carry):
+        new_copy(c).wait()
         wait_all(send, send_sem, c)
         wait_all(back_send, back_send_sem, c)
         return carry
 
     lax.fori_loop(0, chunks, drain, 0)
+
+
+def advect(levs, filtered, speed, speed_ends, out_t, out_s):
+    layers = speed.shape[0]
+    lev = lax.axis_index("lev")
+
+    def level_of(j):
+        w = speed_ends[j // (layers + 1)] if j in (0, layers + 1) else speed[j - 1]
+        return filtered[0, j], filtered[1, j], w
+
+    low = level_of(0)
+    below = None
+    for j in range(layers + 1):
+        high = level_of(j + 1)
+        flow = 0.5 * (low[2] + high[2]) + buoyancy * 0.5 * (
+            (low[0] + high[0]) - (low[1] + high[1])
+        )
+        up, down = jnp.maximum(flow, 0.0), jnp.minimum(flow, 0.0)
+        above = [up * low[f] + down * high[f] for f in range(2)]
+        if j == 0:
+            above = [jnp.where(lev > 0, x, 0.0) for x in above]
+        if j == layers:
+            above = [jnp.where(lev < levs - 1, x, 0.0) for x in above]
+        if j > 0:
+            out_t[j - 1] = low[0] - advective_number * (above[0] - below[0])
+            out_s[j - 1] = low[1] - advective_number * (above[1] - below[1])
+        low, below = high, above
 
 
 def shards(heat, salt, speed, rate_t, rate_s, rate_c):
@@ -369,22 +382,27 @@
     wy2 = np.tile(every * every / scale, (1, 1, pack))
     tables = [jnp.asarray(m) for m in (fwd_y, inv_y, fwd_x, inv_x)]
     tables += [jnp.asarray(m.astype(np.float32)) for m in (wx2, wy2)]
-    vmem = pl.BlockSpec(memory_space=pltpu.VMEM)
     smem = pl.BlockSpec(memory_space=pltpu.SMEM)
     anywhere = pl.BlockSpec(memory_space=pl.ANY)
     block = pltpu.VMEM((chunks, parts, 2, rows, LANES), jnp.float32)
     sems = pltpu.SemaphoreType.DMA((chunks,))
-    shape = jax.ShapeDtypeStruct(heat.shape, jnp.float32)
-    return pl.pallas_call(
+    whole = pltpu.VMEM((2, layers, rows, length_y), jnp.float32)
+    filtered, speed_ends = pl.pallas_call(
         functools.partial(kernel, parts, levs, slots),
-        out_shape=(shape, shape),
-        in_specs=[vmem, vmem, anywhere, smem, smem, smem] + [vmem] * 6,
-        out_specs=(vmem, vmem),
-        scratch_shapes=[
-            block, block, block, block,
-            pltpu.VMEM((3, layers + 2, rows, length_y), jnp.float32),
-            sems, sems, sems, sems,
-            pltpu.SemaphoreType.DMA,
+        out_shape=(
+            jax.ShapeDtypeStruct((2, layers + 2, rows, length_y), jnp.float32),
+            jax.ShapeDtypeStruct((2, rows, length_y), jnp.float32),
+        ),
+        in_specs=[anywhere] * 3 + [smem] * 3 + [anywhere] * 6,
+        out_specs=(anywhere, anywhere),
+        scratch_shapes=[block] * 4
+        + [whole] * 2
+        + [pltpu.VMEM(t.shape, t.dtype) for t in tables]
+        + [sems] * 4
+        + [
+            pltpu.SemaphoreType.DMA((2, chunks)),
+            sems,
+            pltpu.SemaphoreType.DMA((len(tables),)),
             pltpu.SemaphoreType.DMA((2, 2)),
             pltpu.SemaphoreType.DMA((2, 2)),
         ],
@@ -392,6 +410,21 @@
             collective_id=0, has_side_effects=True, vmem_limit_bytes=58 * 2**20
         ),
     )(heat, salt, speed, rate_t, rate_s, rate_c, *tables)
+    wide = min(length_y, 2 * LANES)
+    level = pl.BlockSpec((layers, 8, wide), lambda i, k: (0, i, k))
+    shape = jax.ShapeDtypeStruct(heat.shape, jnp.float32)
+    return pl.pallas_call(
+        functools.partial(advect, levs),
+        grid=(rows // 8, length_y // wide),
+        out_shape=(shape, shape),
+        in_specs=[
+            pl.BlockSpec((2, layers + 2, 8, wide), lambda i, k: (0, 0, i, k)),
+            level,
+            pl.BlockSpec((2, 8, wide), lambda i, k: (0, i, k)),
+        ],
+        out_specs=(level, level),
+        compiler_params=pltpu.CompilerParams(vmem_limit_bytes=32 * 2**20),
+    )(filtered, speed, speed_ends)
 
 
 def solution(mesh):

time: 198 us -> 197 us (level)
    pallas_call x0 -> x1, Pallas kernels: none -> 4.47 us  [shards(): pl.pallas_call(functools.partial(advect, levs), grid=(rows // 8, length_y...]
    pallas_call x1, Pallas kernels: 190 us -> 187 us  [shards(): pl.pallas_call(functools.partial(kernel, parts, levs, slots), out_shape=(...]
    unnamed x4 -> x6, local copies, waits for them, and re-layouts: 4.66 us -> 3.16 us
where the time goes in v2:
time: 197 us; the launch traced here: 195 us
  Pallas kernels  191 us (97%)
  local copies, waits for them, and re-layouts  3.16 us (2%)
    pallas_call x1, Pallas kernels, shards(): pl.pallas_call(functools.partial(kernel, parts, levs, slots), out_shape=(...  187 us
    pallas_call x1, Pallas kernels, shards(): pl.pallas_call(functools.partial(advect, levs), grid=(rows // 8, length_y...  4.47 us

profile of v2, /device:TPU:0, one launch (start us, length us, event | category | flops | bytes accessed | tf_op | source)
XLA Modules:
  0.0 194.8 jit_solution(5998644831013346495)
XLA Ops:
  0.6 0.0 copy-start
  0.6 186.5 %shard_map.131 = (f32[2,34,32,512]{3,2,1,0:T(8,128)}, f32[2,32,512]{2,1,0:T(8,128)}) custom-call(f32[32,32,512]{2,1,0:T(8,128)} %heat.1, f32[32,32,512]{2,1,0:T(8,128)} %salt.1, f32[32,32,512]{2,1,0:T(8,128)} %speed.3, f32[32]{0:T(128)} %rate_t.1, f32[32]{0:T(128)} %rate_s.1, f32[32]{0:T(128)} %rate_c.1, bf16[2,768,256]{2,1,0:T(8,128)(2,1)} %constant.12.clone.rest_0_, ...), custom_call_target="tpu_custom_call" | custom-call | tf_op jit(solution)/shard_map/pallas_call | solution.py:390
  187.2 0.0 copy-done
  187.2 0.0 copy-start.1
  187.2 2.3 %copy-done.1 = f32[2,34,32,512]{3,2,1,0:T(8,128)S(1)} copy-done((f32[2,34,32,512]{3,2,1,0:T(8,128)S(1)}, f32[2,34,32,512]{3,2,1,0:T(8,128)}, u32[]{:S(2)}) %copy-start.1) | copy-done | bytes 4456472
  189.5 0.0 copy-start.2
  189.5 0.9 copy-done.2
  190.4 4.5 %shard_map.132 = (f32[32,32,512]{2,1,0:T(8,128)}, f32[32,32,512]{2,1,0:T(8,128)}) custom-call(f32[2,34,32,512]{3,2,1,0:T(8,128)S(1)} %copy-done.1, f32[32,32,512]{2,1,0:T(8,128)S(1)} %copy-done, f32[2,32,512]{2,1,0:T(8,128)S(1)} %copy-done.2), custom_call_target="tpu_custom_call" | custom-call | tf_op jit(solution)/shard_map/pallas_call | solution.py:416
Async XLA Ops:
  0.6 186.6 %copy-start = (f32[32,32,512]{2,1,0:T(8,128)S(1)}, f32[32,32,512]{2,1,0:T(8,128)}, u32[]{:S(2)}) copy-start(f32[32,32,512]{2,1,0:T(8,128)} %speed.3) | copy-start | bytes 6291460
  187.2 2.3 %copy-start.1 = (f32[2,34,32,512]{3,2,1,0:T(8,128)S(1)}, f32[2,34,32,512]{3,2,1,0:T(8,128)}, u32[]{:S(2)}) copy-start(f32[2,34,32,512]{3,2,1,0:T(8,128)} %get-tuple-element.4.filtered) | copy-start | bytes 13369348
  189.5 0.9 copy-start.2

commit v3 on v2

--- a/solution.py
+++ b/solution.py
@@ -186,9 +186,13 @@
     def lane_of(shape):
         return lax.broadcasted_iota(jnp.int32, shape, 1)
 
+    stride = max(1, parts // 4)
+    while math.gcd(stride, parts - 1) > 1:
+        stride += 1
+
     def exchange(source, target, s_sem, r_sem, c):
-        def one(d, carry):
-            q = peer(d)
+        def one(i, carry):
+            q = peer(1 + lax.rem(i * stride + me, parts - 1))
             pltpu.make_async_remote_copy(
                 src_ref=source.at[c, q],
                 dst_ref=target.at[c, me],
@@ -423,7 +427,7 @@
             pl.BlockSpec((2, 8, wide), lambda i, k: (0, i, k)),
         ],
         out_specs=(level, level),
-        compiler_params=pltpu.CompilerParams(vmem_limit_bytes=32 * 2**20),
+        compiler_params=pltpu.CompilerParams(vmem_limit_bytes=58 * 2**20),
     )(filtered, speed, speed_ends)
 
 

time: 197 us -> 198 us (level)
  Pallas kernels: 191 us -> 197 us
  local copies, waits for them, and re-layouts: 3.16 us -> 0 us
    pallas_call x1, Pallas kernels: 4.47 us -> 7.66 us  [shards(): pl.pallas_call(functools.partial(advect, levs), grid=(rows // 8, length_y...]
    unnamed x6 -> x0, local copies, waits for them, and re-layouts: 3.16 us -> none
    pallas_call x1, Pallas kernels: 187 us -> 189 us  [shards(): pl.pallas_call(functools.partial(kernel, parts, levs, slots), out_shape=(...]
where the time goes in v3:
time: 198 us; the launch traced here: 197 us
  Pallas kernels  197 us (99%)
    pallas_call x1, Pallas kernels, shards(): pl.pallas_call(functools.partial(kernel, parts, levs, slots), out_shape=(...  189 us
    pallas_call x1, Pallas kernels, shards(): pl.pallas_call(functools.partial(advect, levs), grid=(rows // 8, length_y...  7.66 us

profile of v3, /device:TPU:0, one launch (start us, length us, event | category | flops | bytes accessed | tf_op | source)
XLA Modules:
  0.0 197.5 jit_solution(1925865416199574065)
XLA Ops:
  0.6 189.2 %shard_map.131 = (f32[2,34,32,512]{3,2,1,0:T(8,128)}, f32[2,32,512]{2,1,0:T(8,128)}) custom-call(f32[32,32,512]{2,1,0:T(8,128)} %heat.1, f32[32,32,512]{2,1,0:T(8,128)} %salt.1, f32[32,32,512]{2,1,0:T(8,128)} %speed.3, f32[32]{0:T(128)} %rate_t.1, f32[32]{0:T(128)} %rate_s.1, f32[32]{0:T(128)} %rate_c.1, bf16[2,768,256]{2,1,0:T(8,128)(2,1)} %constant.12.clone.rest_0_, ...), custom_call_target="tpu_custom_call" | custom-call | tf_op jit(solution)/shard_map/pallas_call | solution.py:394
  189.8 7.7 %shard_map.132 = (f32[32,32,512]{2,1,0:T(8,128)}, f32[32,32,512]{2,1,0:T(8,128)}) custom-call(f32[2,34,32,512]{3,2,1,0:T(8,128)} %get-tuple-element.4.filtered, f32[32,32,512]{2,1,0:T(8,128)} %speed.3, f32[2,32,512]{2,1,0:T(8,128)} %get-tuple-element.5.speed_ends), custom_call_target="tpu_custom_call" | custom-call | tf_op jit(solution)/shard_map/pallas_call | solution.py:420

commit v4 on v2

--- a/solution.py
+++ b/solution.py
@@ -339,10 +339,11 @@
 def advect(levs, filtered, speed, speed_ends, out_t, out_s):
     layers = speed.shape[0]
     lev = lax.axis_index("lev")
+    r = pl.ds(pl.multiple_of(pl.program_id(0) * 8, 8), 8)
 
     def level_of(j):
-        w = speed_ends[j // (layers + 1)] if j in (0, layers + 1) else speed[j - 1]
-        return filtered[0, j], filtered[1, j], w
+        w = speed_ends[j // (layers + 1), r] if j in (0, layers + 1) else speed[j - 1, r]
+        return filtered[0, j, r], filtered[1, j, r], w
 
     low = level_of(0)
     below = None
@@ -390,8 +391,8 @@
     filtered, speed_ends = pl.pallas_call(
         functools.partial(kernel, parts, levs, slots),
         out_shape=(
-            jax.ShapeDtypeStruct((2, layers + 2, rows, length_y), jnp.float32),
-            jax.ShapeDtypeStruct((2, rows, length_y), jnp.float32),
+            pltpu.VMEM((2, layers + 2, rows, length_y), jnp.float32),
+            pltpu.VMEM((2, rows, length_y), jnp.float32),
         ),
         in_specs=[anywhere] * 3 + [smem] * 3 + [anywhere] * 6,
         out_specs=(anywhere, anywhere),
@@ -407,23 +408,19 @@
             pltpu.SemaphoreType.DMA((2, 2)),
         ],
         compiler_params=pltpu.CompilerParams(
-            collective_id=0, has_side_effects=True, vmem_limit_bytes=58 * 2**20
+            collective_id=0, has_side_effects=True, vmem_limit_bytes=57 * 2**20
         ),
     )(heat, salt, speed, rate_t, rate_s, rate_c, *tables)
-    wide = min(length_y, 2 * LANES)
-    level = pl.BlockSpec((layers, 8, wide), lambda i, k: (0, i, k))
+    level = pl.BlockSpec((layers, 8, length_y), lambda i: (0, i, 0))
+    whole = pl.BlockSpec(memory_space=pltpu.VMEM)
     shape = jax.ShapeDtypeStruct(heat.shape, jnp.float32)
     return pl.pallas_call(
         functools.partial(advect, levs),
-        grid=(rows // 8, length_y // wide),
+        grid=(rows // 8,),
         out_shape=(shape, shape),
-        in_specs=[
-            pl.BlockSpec((2, layers + 2, 8, wide), lambda i, k: (0, 0, i, k)),
-            level,
-            pl.BlockSpec((2, 8, wide), lambda i, k: (0, i, k)),
-        ],
+        in_specs=[whole] * 3,
         out_specs=(level, level),
-        compiler_params=pltpu.CompilerParams(vmem_limit_bytes=32 * 2**20),
+        compiler_params=pltpu.CompilerParams(vmem_limit_bytes=16 * 2**20),
     )(filtered, speed, speed_ends)
 
 

time: 197 us -> 192 us (0.975)
  local copies, waits for them, and re-layouts: 3.16 us -> 0.01 us
  Pallas kernels: 191 us -> 189 us
    unnamed x6 -> x2, local copies, waits for them, and re-layouts: 3.16 us -> 0.01 us
where the time goes in v4:
time: 192 us; the launch traced here: 190 us
  Pallas kernels  189 us (98%)
    pallas_call x1, Pallas kernels, shards(): pl.pallas_call(functools.partial(kernel, parts, levs, slots), out_shape=(...  186 us

profile of v4, /device:TPU:0, one launch (start us, length us, event | category | flops | bytes accessed | tf_op | source)
XLA Modules:
  0.0 189.6 jit_solution(4964105049731584857)
XLA Ops:
  0.6 0.0 copy-start
  0.6 185.8 %shard_map.131 = (f32[2,34,32,512]{3,2,1,0:T(8,128)S(1)}, f32[2,32,512]{2,1,0:T(8,128)S(1)}) custom-call(f32[32,32,512]{2,1,0:T(8,128)} %heat.1, f32[32,32,512]{2,1,0:T(8,128)} %salt.1, f32[32,32,512]{2,1,0:T(8,128)} %speed.3, f32[32]{0:T(128)} %rate_t.1, f32[32]{0:T(128)} %rate_s.1, f32[32]{0:T(128)} %rate_c.1, ...), custom_call_target="tpu_custom_call" | custom-call | tf_op jit(solution)/shard_map/pallas_call | solution.py:391
  186.5 0.0 copy-done
  186.5 3.1 %shard_map.132 = (f32[32,32,512]{2,1,0:T(8,128)}, f32[32,32,512]{2,1,0:T(8,128)}) custom-call(f32[2,34,32,512]{3,2,1,0:T(8,128)S(1)} %get-tuple-element.4.filtered, f32[32,32,512]{2,1,0:T(8,128)S(1)} %copy-done, f32[2,32,512]{2,1,0:T(8,128)S(1)} %get-tuple-element.5.speed_ends), custom_call_target="tpu_custom_call" | custom-call | tf_op jit(solution)/shard_map/pallas_call | solution.py:417
Async XLA Ops:
  0.6 185.9 %copy-start = (f32[32,32,512]{2,1,0:T(8,128)S(1)}, f32[32,32,512]{2,1,0:T(8,128)}, u32[]{:S(2)}) copy-start(f32[32,32,512]{2,1,0:T(8,128)} %speed.3) | copy-start | bytes 6291460

commit v5 on v4

--- a/solution.py
+++ b/solution.py
@@ -187,8 +187,8 @@
         return lax.broadcasted_iota(jnp.int32, shape, 1)
 
     def exchange(source, target, s_sem, r_sem, c):
-        def one(d, carry):
-            q = peer(d)
+        def one(i, carry):
+            q = peer(jnp.where(i <= parts // 2, parts // 2 + i - 1, parts - i))
             pltpu.make_async_remote_copy(
                 src_ref=source.at[c, q],
                 dst_ref=target.at[c, me],
@@ -316,6 +316,7 @@
         wait_all(back_recv, back_recv_sem, c)
         south(c)
         new_copy(c).start()
+        wait_all(send, send_sem, c)
 
         @pl.when(i == 1)
         def _():
@@ -329,7 +330,6 @@
 
     def drain(c, carry):
         new_copy(c).wait()
-        wait_all(send, send_sem, c)
         wait_all(back_send, back_send_sem, c)
         return carry
 

time: 192 us -> 194 us (1.010); the launches traced: 190 us -> 194 us
  Pallas kernels: 189 us -> 193 us
    pallas_call x1, Pallas kernels: 186 us -> 190 us  [shards(): pl.pallas_call(functools.partial(kernel, parts, levs, slots), out_shape=(...]
where the time goes in v5:
time: 194 us
  Pallas kernels  193 us (99%)
    pallas_call x1, Pallas kernels, shards(): pl.pallas_call(functools.partial(kernel, parts, levs, slots), out_shape=(...  190 us

profile of v5, /device:TPU:0, one launch (start us, length us, event | category | flops | bytes accessed | tf_op | source)
XLA Modules:
  0.0 193.7 jit_solution(7372638508186995318)
XLA Ops:
  0.6 0.0 copy-start
  0.6 189.9 %shard_map.131 = (f32[2,34,32,512]{3,2,1,0:T(8,128)S(1)}, f32[2,32,512]{2,1,0:T(8,128)S(1)}) custom-call(f32[32,32,512]{2,1,0:T(8,128)} %heat.1, f32[32,32,512]{2,1,0:T(8,128)} %salt.1, f32[32,32,512]{2,1,0:T(8,128)} %speed.3, f32[32]{0:T(128)} %rate_t.1, f32[32]{0:T(128)} %rate_s.1, f32[32]{0:T(128)} %rate_c.1, ...), custom_call_target="tpu_custom_call" | custom-call | tf_op jit(solution)/shard_map/pallas_call | solution.py:391
  190.6 0.0 copy-done
  190.6 3.1 %shard_map.132 = (f32[32,32,512]{2,1,0:T(8,128)}, f32[32,32,512]{2,1,0:T(8,128)}) custom-call(f32[2,34,32,512]{3,2,1,0:T(8,128)S(1)} %get-tuple-element.4.filtered, f32[32,32,512]{2,1,0:T(8,128)S(1)} %copy-done, f32[2,32,512]{2,1,0:T(8,128)S(1)} %get-tuple-element.5.speed_ends), custom_call_target="tpu_custom_call" | custom-call | tf_op jit(solution)/shard_map/pallas_call | solution.py:417
Async XLA Ops:
  0.6 190.0 %copy-start = (f32[32,32,512]{2,1,0:T(8,128)S(1)}, f32[32,32,512]{2,1,0:T(8,128)}, u32[]{:S(2)}) copy-start(f32[32,32,512]{2,1,0:T(8,128)} %speed.3) | copy-start | bytes 6291460

commit v6 on v4

--- a/solution.py
+++ b/solution.py
@@ -188,7 +188,7 @@
 
     def exchange(source, target, s_sem, r_sem, c):
         def one(d, carry):
-            q = peer(d)
+            q = peer(parts - d)
             pltpu.make_async_remote_copy(
                 src_ref=source.at[c, q],
                 dst_ref=target.at[c, me],

time: 192 us -> 194 us (1.010); the launches traced: 190 us -> 194 us
  Pallas kernels: 189 us -> 193 us
    pallas_call x1, Pallas kernels: 186 us -> 190 us  [shards(): pl.pallas_call(functools.partial(kernel, parts, levs, slots), out_shape=(...]
where the time goes in v6:
time: 194 us
  Pallas kernels  193 us (99%)
    pallas_call x1, Pallas kernels, shards(): pl.pallas_call(functools.partial(kernel, parts, levs, slots), out_shape=(...  190 us

profile of v6, /device:TPU:0, one launch (start us, length us, event | category | flops | bytes accessed | tf_op | source)
XLA Modules:
  0.0 193.9 jit_solution(1011141223241417902)
XLA Ops:
  0.6 0.0 copy-start
  0.6 190.2 %shard_map.131 = (f32[2,34,32,512]{3,2,1,0:T(8,128)S(1)}, f32[2,32,512]{2,1,0:T(8,128)S(1)}) custom-call(f32[32,32,512]{2,1,0:T(8,128)} %heat.1, f32[32,32,512]{2,1,0:T(8,128)} %salt.1, f32[32,32,512]{2,1,0:T(8,128)} %speed.3, f32[32]{0:T(128)} %rate_t.1, f32[32]{0:T(128)} %rate_s.1, f32[32]{0:T(128)} %rate_c.1, ...), custom_call_target="tpu_custom_call" | custom-call | tf_op jit(solution)/shard_map/pallas_call | solution.py:391
  190.8 0.0 copy-done
  190.8 3.1 %shard_map.132 = (f32[32,32,512]{2,1,0:T(8,128)}, f32[32,32,512]{2,1,0:T(8,128)}) custom-call(f32[2,34,32,512]{3,2,1,0:T(8,128)S(1)} %get-tuple-element.4.filtered, f32[32,32,512]{2,1,0:T(8,128)S(1)} %copy-done, f32[2,32,512]{2,1,0:T(8,128)S(1)} %get-tuple-element.5.speed_ends), custom_call_target="tpu_custom_call" | custom-call | tf_op jit(solution)/shard_map/pallas_call | solution.py:417
Async XLA Ops:
  0.6 190.2 %copy-start = (f32[32,32,512]{2,1,0:T(8,128)S(1)}, f32[32,32,512]{2,1,0:T(8,128)}, u32[]{:S(2)}) copy-start(f32[32,32,512]{2,1,0:T(8,128)} %speed.3) | copy-start | bytes 6291460
